TPU v7x, 32 devices: a whole 2x2x4 slice. The times are simulated.
32 devices in a mesh: sub: 8 (over z, core), hgt: 4 (over y, x).
Axes of the slice: x: 2, y: 2, z: 4, core: 2. Of those that a mesh axis runs over, the one named last changes fastest.
Arguments:
- polar_beams: bfloat16 [4, 2, 128, 4096], P('hgt', None, 'sub'), may hold values from -6 to 6
- band_start: int32 [3, 2, 2, 16], replicated, may hold values from 0 to 8, as said below
- band_weight: bfloat16 [3, 2, 2, 16, 8], replicated, may hold values from -1.5 to 1.5
- phase_rate: float32 [3, 2, 2, 16], replicated, may hold values from -6 to 6
- layer_wave: float32 [4], P('hgt'), may hold values from 0.5 to 2
- beam_map: int32 [16, 2048], replicated, may hold values from 0 to 126, as said below
- range_map: int32 [16, 2048], replicated, may hold values from 0 to 4094
- pixel_frac: bfloat16 [3, 16, 2048], replicated, may hold values from 0 to 1
Outputs:
- image: float32 [16, 4, 2, 2048], P('sub', 'hgt')
Inputs may be any that keep to these rules, and one draw needn't show every extreme that they name: band_start[l,k,h,j] + t for t < 8 lies within h * 8 - 8 to h * 8 + 16 / 2 + 7. beam_map[y, x] differs from x * 128 // 2048 by at most 2.
All inputs are finite; a program needn't handle non-finite values.
Results may differ from a plain program's by a relative error of at most 0.0041.
Values may be sent and summed in bfloat16 or wider, within the bound.
A program may use at most 192 MiB of HBM per device.

v0:
```python
import jax
import jax.numpy as jnp
from jax import lax
from jax.sharding import PartitionSpec as P

range_phase = 0.003


def from_partner(value, axis, bit):
    mask = 2**bit
    pairs = [(source, source ^ mask) for source in range(lax.axis_size(axis))]
    return lax.ppermute(value, axis, pairs)


def from_behind(block, axis, distance):
    devices = range(lax.axis_size(axis))
    route = [(i - distance, i) for i in devices if i - distance in devices]
    return lax.ppermute(block, axis, route)


def rotate(real_part, imag_part, angles):
    cosine = jnp.cos(angles)
    sine_part = jnp.sin(angles)
    return (cosine * real_part - sine_part * imag_part, sine_part * real_part + cosine * imag_part)


def band_matrix(starts, weights, first_row, row_total):
    col_ids = jnp.arange(row_total, dtype=jnp.int32) + first_row
    tap_ids = jnp.arange(weights.shape[-1], dtype=jnp.int32)
    matches = (col_ids[None, None, :] == starts[:, None, None] + tap_ids[None, :, None]).astype(
        jnp.float32
    )
    return jnp.einsum("jt,jtc->jc", weights.astype(jnp.float32), matches).astype(jnp.bfloat16)


def contribution(layer_beams, matrix, angles):
    blended = jnp.einsum("jc,zpcr->zpjr", matrix, layer_beams, preferred_element_type=jnp.float32)
    real_part, imag_part = rotate(blended[:, 0], blended[:, 1], angles)
    return jnp.stack([real_part, imag_part], axis=1)


def body(
    polar_beams, band_start, band_weight, phase_rate, layer_wave, beam_map, range_map, pixel_frac
):
    sub_index = lax.axis_index("sub")
    sub_count = lax.axis_size("sub")
    layer_count = polar_beams.shape[0]
    beam_count = polar_beams.shape[2]
    range_count = polar_beams.shape[3]
    levels = band_start.shape[0]
    column_count = beam_map.shape[1]
    range_pos = (jnp.arange(range_count, dtype=jnp.float32) + 0.5) / range_count

    def phase_angles(section, child, my_half):
        return (
            layer_wave[:, None, None]
            * phase_rate[section][child, my_half][None, :, None]
            * range_pos[None, None, :]
        )

    def merge_section(current, section):
        my_half = sub_index >> section & 1
        far_half = 1 - my_half
        own_part = contribution(
            current,
            band_matrix(
                band_start[section][my_half, my_half],
                band_weight[section][my_half, my_half],
                0,
                beam_count,
            ),
            phase_angles(section, my_half, my_half),
        )
        received = from_partner(current, "sub", section)
        first_row = 0
        far_part = contribution(
            received,
            band_matrix(
                band_start[section][far_half, my_half],
                band_weight[section][far_half, my_half],
                first_row,
                beam_count,
            ),
            phase_angles(section, far_half, my_half),
        )
        return own_part + far_part

    current = polar_beams
    for section in range(levels - 1):
        current = merge_section(current, section).astype(jnp.bfloat16)
    final_polar = merge_section(current, levels - 1)
    sector_idx = jnp.int32(0)
    for bit_idx in range(levels):
        sector_idx = sector_idx * 2 + (sub_index >> bit_idx & 1)
    sector_start = sector_idx * beam_count
    flat_polar = final_polar.reshape(layer_count, 2, beam_count * range_count)
    cols_per_beam = column_count // (beam_count * 2**levels)
    window = min(column_count, ((beam_count + 5) * cols_per_beam + 127) // 128 * 128)
    col_start = jnp.clip((sector_start - 3) * cols_per_beam, 0, column_count - window)
    tile_rows = beam_map.shape[0] // sub_count
    pixel_rows = tile_rows * lax.axis_size("sub")
    rows_beam = lax.dynamic_slice(beam_map, (0, col_start), (pixel_rows, window))
    rows_range = lax.dynamic_slice(range_map, (0, col_start), (pixel_rows, window))
    beam_frac = lax.dynamic_slice(pixel_frac[0], (0, col_start), (pixel_rows, window)).astype(
        jnp.float32
    )
    range_frac = lax.dynamic_slice(pixel_frac[1], (0, col_start), (pixel_rows, window)).astype(
        jnp.float32
    )
    summed = jnp.zeros((layer_count, 2, pixel_rows * window), jnp.float32)
    for beam_step in range(2):
        local_beam = rows_beam + beam_step - sector_start
        inside = (local_beam >= 0) & (local_beam < beam_count)
        beam_part = jnp.where(inside, beam_frac if beam_step else 1.0 - beam_frac, 0.0)
        clipped = jnp.clip(local_beam, 0, beam_count - 1)
        for range_step in range(2):
            pair_weight = beam_part * (range_frac if range_step else 1.0 - range_frac)
            flat_index = (clipped * range_count + rows_range + range_step).reshape(-1)
            summed = summed + pair_weight.reshape(-1)[None, None, :] * jnp.take(
                flat_polar, flat_index, axis=2
            )
    angles = (
        layer_wave[:, None]
        * range_phase
        * (rows_range.astype(jnp.float32) + range_frac).reshape(-1)[None, :]
    )
    real_part, imag_part = rotate(summed[:, 0], summed[:, 1], angles)
    stacked = jnp.stack([real_part, imag_part], axis=1).reshape(layer_count, 2, pixel_rows, window)
    placed = jnp.zeros((layer_count, 2, pixel_rows, column_count), jnp.float32)
    placed = lax.dynamic_update_slice(
        placed, stacked, (jnp.int32(0), jnp.int32(0), jnp.int32(0), col_start)
    )
    my_tile = lax.psum_scatter(
        jnp.transpose(placed, (2, 0, 1, 3)), "sub", scatter_dimension=0, tiled=True
    )
    above_layer = from_behind(my_tile, "hgt", -1)
    upper_layers = jnp.concatenate([my_tile[:, 1:], above_layer], axis=1)
    height_frac = lax.dynamic_slice_in_dim(
        pixel_frac[2], sub_index * tile_rows, tile_rows, 0
    ).astype(jnp.float32)[:, None, None, :]
    return (1.0 - height_frac) * my_tile + height_frac * upper_layers


def solution(mesh):
    in_specs = (P("hgt", None, "sub", None), P(), P(), P(), P("hgt"), P(), P(), P())
    out_specs = P("sub", "hgt", None, None)
    return jax.shard_map(body, mesh=mesh, in_specs=in_specs, out_specs=out_specs, check_vma=False)
```

profile of v0, /device:TPU:0, one launch (start us, length us, event | category | flops | bytes accessed | tf_op | source)
XLA Modules:
  0.0 302.5 jit_solution(15449913306806193651)
XLA Ops:
  6.5 0.5 collective-permute-start
  7.0 0.9 broadcast_add_fusion.1
  8.0 0.6 compare_and_fusion
  8.6 0.6 compare_and_fusion.2
  9.2 0.7 fusion.114
  10.1 0.7 fusion.116
  11.0 0.2 fusion.46
  11.2 1.2 convolution_bitcast_fusion.5
  13.0 0.7 fusion.115
  14.1 0.9 fusion.113
  15.0 0.2 fusion.47
  15.2 0.2 fusion.48
  15.5 0.2 fusion.49
  15.7 0.9 fusion.66
  16.7 0.9 convert_multiply_fusion.1
  17.9 2.1 fusion.32
  20.0 2.6 collective-permute-start.1
  23.2 6.4 %collective-permute-done.1 = bf16[1,2,16,4096]{3,2,1,0:T(8,128)(2,1)S(1)} collective-permute-done((bf16[1,2,16,4096]{3,2,1,0:T(8,128)(2,1)S(1)}, bf16[1,2,16,4096]{3,2,1,0:T(8,128)(2,1)S(1)}, u32[]{:S(2)}, u32[]{:S(2)}) %collective-permute-start.1) | collective-permute-done | bytes 262176 | tf_op jit(solution)/shard_map/ppermute | solution.py:12
  29.9 2.1 fusion.30
  32.0 2.8 collective-permute-start.2
  35.2 0.6 dynamic-slice.21
  36.7 10.1 %collective-permute-done.2 = bf16[1,2,16,4096]{3,2,1,0:T(8,128)(2,1)S(1)} collective-permute-done((bf16[1,2,16,4096]{3,2,1,0:T(8,128)(2,1)S(1)}, bf16[1,2,16,4096]{3,2,1,0:T(8,128)(2,1)S(1)}, u32[]{:S(2)}, u32[]{:S(2)}) %collective-permute-start.2) | collective-permute-done | bytes 262176 | tf_op jit(solution)/shard_map/ppermute | solution.py:12
  47.0 2.1 fusion.28
  49.1 0.3 stack.90
  49.4 0.3 stack.91
  49.7 0.5 pad_maximum_fusion.1
  50.2 15.6 %copy.32 = f32[1,2,65536]{1,2,0:T(8,128)} copy(f32[1,2,65536]{2,1,0:T(2,128)S(1)} %pad_maximum_fusion.1) | data formatting | bytes 1048576 | tf_op jit(solution)/shard_map/stack | solution.py:39
  65.8 0.3 stack.85
  66.1 0.3 stack.86
  66.5 0.5 pad_maximum_fusion
  66.9 15.4 %copy.31 = f32[1,2,65536]{1,2,0:T(8,128)} copy(f32[1,2,65536]{2,1,0:T(2,128)S(1)} %pad_maximum_fusion) | data formatting | bytes 1048576 | tf_op jit(solution)/shard_map/stack | solution.py:39
  82.4 33.3 %add_bitcast_fusion = f32[2,65536]{0,1:T(8,128)} fusion(f32[1,2,65536]{1,2,0:T(8,128)} %copy.31, f32[1,2,65536]{1,2,0:T(8,128)} %copy.32), kind=kLoop, calls=%fused_computation.4 | loop fusion | flops 131072 | bytes 1572864 | tf_op jit(solution)/shard_map/jit(_take)/Arg_0.9 | solution.py:119
  115.7 26.6 %gather_fusion = f32[6144,2]{1,0:T(8,128)S(1)} fusion(f32[2,65536]{0,1:T(8,128)} %add_bitcast_fusion, s32[6144]{0:T(1024)S(1)} %fusion.69), kind=kCustom, calls=%fused_computation.clone | custom fusion | bytes 122880 | tf_op jit(solution)/shard_map/jit(_take)/gather | solution.py:119
  142.3 1.2 copy.33
  143.5 26.6 %gather_fusion.1 = f32[6144,2]{1,0:T(8,128)S(1)} fusion(f32[2,65536]{0,1:T(8,128)} %add_bitcast_fusion, s32[6144]{0:T(1024)S(1)} %fusion.70), kind=kCustom, calls=%fused_computation.1.clone | custom fusion | bytes 122880 | tf_op jit(solution)/shard_map/jit(_take)/gather | solution.py:119
  170.1 1.2 copy.34
  171.3 26.6 %gather_fusion.2 = f32[6144,2]{1,0:T(8,128)S(1)} fusion(f32[2,65536]{0,1:T(8,128)} %add_bitcast_fusion, s32[6144]{0:T(1024)S(1)} %fusion.71), kind=kCustom, calls=%fused_computation.2.clone | custom fusion | bytes 122880 | tf_op jit(solution)/shard_map/jit(_take)/gather | solution.py:119
  197.9 1.2 copy.35
  199.1 26.6 %gather_fusion.3 = f32[6144,2]{1,0:T(8,128)S(1)} fusion(f32[2,65536]{0,1:T(8,128)} %add_bitcast_fusion, s32[6144]{0:T(1024)S(1)} %fusion.72), kind=kCustom, calls=%fused_computation.3.clone | custom fusion | bytes 122880 | tf_op jit(solution)/shard_map/jit(_take)/gather | solution.py:119
  225.8 1.2 copy.36
  226.9 0.9 fusion.53
  228.2 0.4 dynamic_update_slice.3
  228.7 0.7 copy-done
  229.4 58.3 %all-reduce.3.cloned.1.call-done = f32[16,1,2,2048]{3,2,1,0:T(2,128)} async-done(((f32[16,1,2,2048]{3,2,1,0:T(2,128)}), f32[16,1,2,2048]{3,2,1,0:T(2,128)}) %all-reduce.3.cloned.1.call-update) | async-done | bytes 262160
  287.7 0.8 constant_dynamic-slice_fusion.19
  288.4 1.3 collective-permute-start.3
  289.8 4.5 %collective-permute-done.3 = f32[2,1,2,2048]{3,2,1,0:T(2,128)S(1)} collective-permute-done((f32[2,1,2,2048]{3,2,1,0:T(2,128)S(1)}, f32[2,1,2,2048]{3,2,1,0:T(2,128)S(1)}, u32[]{:S(2)}, u32[]{:S(2)}) %collective-permute-start.3) | collective-permute-done | bytes 32800 | tf_op jit(solution)/shard_map/ppermute | solution.py:18
  294.2 1.4 multiply_add_fusion
  (56 shorter events, 3.0 us)
Async XLA Ops:
  6.5 281.2 %all-reduce.3.cloned.1.call-start = ((), (), s32[]{:S(2)}) async-start(), calls=%async_computation | async-start | bytes 524288
  6.5 11.1 %collective-permute-start = (bf16[1,2,16,4096]{3,2,1,0:T(8,128)(2,1)}, bf16[1,2,16,4096]{3,2,1,0:T(8,128)(2,1)S(1)}, u32[]{:S(2)}, u32[]{:S(2)}) collective-permute-start(bf16[1,2,16,4096]{3,2,1,0:T(8,128)(2,1)} %param.10), channel_id=1, source_target_pairs={{0,4},{4,0},{8,12},{12,8},{16,20},{20,16},{24,28},{28,24},{1,5},{5... | collective-permute-start | bytes 786440 | tf_op jit(solution)/shard_map/ppermute | solution.py:12
  20.0 9.6 %collective-permute-start.1 = (bf16[1,2,16,4096]{3,2,1,0:T(8,128)(2,1)S(1)}, bf16[1,2,16,4096]{3,2,1,0:T(8,128)(2,1)S(1)}, u32[]{:S(2)}, u32[]{:S(2)}) collective-permute-start(bf16[1,2,16,4096]{3,2,1,0:T(8,128)(2,1)S(1)} %fusion.2), channel_id=1, source_target_pairs={{0,8},{4,12},{8,0},{12,4},{16,24},{20,28},{24,16},{28,20},{1,9},{5... | collective-permute-start | bytes 786440 | tf_op jit(solution)/shard_map/ppermute | solution.py:12
  23.0 12.2 %copy-start.1 = (u32[32]{0:T(128)S(1)}, u32[32]{0:T(128)}, u32[]{:S(2)}) copy-start(u32[32]{0:T(128)} %constant.81) | copy-start | bytes 388
  32.0 14.7 %collective-permute-start.2 = (bf16[1,2,16,4096]{3,2,1,0:T(8,128)(2,1)S(1)}, bf16[1,2,16,4096]{3,2,1,0:T(8,128)(2,1)S(1)}, u32[]{:S(2)}, u32[]{:S(2)}) collective-permute-start(bf16[1,2,16,4096]{3,2,1,0:T(8,128)(2,1)S(1)} %fusion.3), channel_id=1, source_target_pairs={{0,16},{4,20},{8,24},{12,28},{16,0},{20,4},{24,8},{28,12},{1,17},{... | collective-permute-start | bytes 786440 | tf_op jit(solution)/shard_map/ppermute | solution.py:12
  228.7 0.7 copy-start
  288.4 5.8 %collective-permute-start.3 = (f32[2,1,2,2048]{3,2,1,0:T(2,128)S(1)}, f32[2,1,2,2048]{3,2,1,0:T(2,128)S(1)}, u32[]{:S(2)}, u32[]{:S(2)}) collective-permute-start(f32[2,1,2,2048]{3,2,1,0:T(2,128)S(1)} %constant_dynamic-slice_fusion.19), channel_id=1, source_target_pairs={{1,0},{2,1},{3,2},{5,4},{6,5},{7,6},{9,8},{10,9},{11,10},{13,12},{... | collective-permute-start | bytes 98312 | tf_op jit(solution)/shard_map/ppermute | solution.py:18
Sparse Core Ops, SparseCore 0:
  229.5 58.1 all-reduce.2
where the time goes:
time: 303 us; the launch traced here: 302 us
  local copies, waits for them, and re-layouts  150 us (50%)
  waiting for transfers between devices  79.3 us (26%)
  other arithmetic  47.6 us (16%)
  between operations  15.1 us (5%)
  starting transfers between devices  7.2 us (2%)
  matrix products  3.42 us (1%)
    gather x8, local copies, waits for them, and re-layouts, body(): jnp.take(flat_polar, flat_index, axis=2)  111 us
    unnamed x2, waiting for transfers between devices  58.3 us
    another operation x1, other arithmetic, body(): jnp.take(flat_polar, flat_index, axis=2)  33.3 us
    another operation x6, local copies, waits for them, and re-layouts, contribution(): return jnp.stack([real_part, imag_part], axis=1)  32.3 us
    ppermute x3, waiting for transfers between devices, from_partner(): return lax.ppermute(value, axis, pairs)  16.5 us
    sub x4, other arithmetic, rotate(): cosine * real_part - sine_part * imag_part  6.47 us
  transfers between devices with their start and end apart: 5, of which 4 were waited for; matrix products, arithmetic and copies ran while one was open for 4% of the time, Pallas kernels for 0%

commit v1 on v0

v1 whole, which is shorter than its diff:
```python
import functools

import jax
import jax.numpy as jnp
from jax import lax
from jax.experimental import pallas as pl
from jax.experimental.pallas import tpu as pltpu
from jax.sharding import PartitionSpec as P

range_phase = 0.003
LANES = 128
SLOT = 256
MESH = pl.DeviceIdType.MESH
VMEM = pltpu.VMEM


def sincos(x):
    q = jnp.floor(x * 0.6366197723675814 + 0.5)
    y = x - q * 1.5703125
    y = y - q * 4.837512969970703e-4
    y = y - q * 7.549789948768648e-8
    z = y * y
    s = y + y * z * (-1.6666654611e-1 + z * (8.3321608736e-3 + z * -1.9515295891e-4))
    c = 1.0 - 0.5 * z + z * z * (
        4.166664568298827e-2 + z * (-1.388731625493765e-3 + z * 2.443315711809948e-5)
    )
    n = q.astype(jnp.int32)
    odd = (n & 1) == 1
    sin_ = jnp.where(odd, c, s)
    cos_ = jnp.where(odd, s, c)
    sin_ = jnp.where((n & 2) == 2, -sin_, sin_)
    cos_ = jnp.where(((n + 1) & 2) == 2, -cos_, cos_)
    return sin_, cos_


def reverse_bits(value, width):
    result = 0
    for bit in range(width):
        result = result * 2 + ((value >> bit) & 1)
    return result


def iota(shape, dim):
    return lax.broadcasted_iota(jnp.int32, shape, dim)


def spread(out_ref, values):
    for y in range(values.shape[0]):
        out_ref[y] = values[y : y + 1].astype(out_ref.dtype)


def column_of(row, size):
    eye = iota((size, size), 0) == iota((size, size), 1)
    return jnp.sum(jnp.where(eye, row, 0.0), axis=1, keepdims=True)


def exchange_kernel(group, polar_ref, out_ref, send_sem, recv_sem, own_sem):
    me = lax.axis_index("sub")
    place = lax.rem(me, group)
    base = me - place
    chunk = out_ref.shape[-1]

    def columns(index):
        return pl.ds(pl.multiple_of(index * chunk, chunk), chunk)

    barrier = pltpu.get_barrier_semaphore()
    for i in range(1, group):
        pl.semaphore_signal(
            barrier, inc=1, device_id={"sub": base + lax.rem(place + i, group)}, device_id_type=MESH
        )
    pl.semaphore_wait(barrier, group - 1)
    own = pltpu.make_async_copy(polar_ref.at[0, :, :, columns(place)], out_ref.at[place], own_sem)
    copies = []
    for i in range(1, group):
        there = lax.rem(place + i, group)
        copies.append(
            pltpu.make_async_remote_copy(
                src_ref=polar_ref.at[0, :, :, columns(there)],
                dst_ref=out_ref.at[place],
                send_sem=send_sem.at[i],
                recv_sem=recv_sem.at[i],
                device_id={"sub": base + there},
                device_id_type=MESH,
            )
        )
        copies[-1].start()
    own.start()
    own.wait()
    for copy in copies:
        copy.wait()


def tables(levels, beams, first, total, wave, start_ref, weight_ref, rate_ref, m_ref, cos_ref, sin_ref):
    group = 2**levels
    width = group * beams
    chunk = cos_ref.shape[-1]
    lane = iota((beams, width), 1)
    lane_beam = (lane % beams).astype(jnp.float32)
    lane_sub = lane // beams
    pos = (iota((1, chunk), 1).astype(jnp.float32) + first + 0.5) / total
    for l in range(levels):
        for k in range(2):
            for h in range(2):
                start = column_of(start_ref[l, k, h : h + 1].astype(jnp.float32), beams)
                weight = weight_ref[l, k, h].astype(jnp.float32)
                band = jnp.zeros((beams, width), jnp.float32)
                for t in range(weight.shape[1]):
                    band = jnp.where(lane_beam == start + t, weight[:, t : t + 1], band)
                for s in range(group):
                    if (s >> l) & 1 == h:
                        child = (s & ~(1 << l)) | (k << l)
                        m_ref[l, pl.ds((k * group + s) * beams, beams), :] = jnp.where(
                            lane_sub == child, band, 0.0
                        ).astype(jnp.bfloat16)
                rate = column_of(rate_ref[l, k, h : h + 1], beams)
                sine, cosine = sincos(wave * rate * pos)
                cos_ref[l, k, h] = cosine
                sin_ref[l, k, h] = sine


def merge(levels, beams, x_ref, cur_ref, y_ref, m_ref, cos_ref, sin_ref):
    group = 2**levels
    width = group * beams
    chunk = x_ref.shape[-1]
    for s in range(group):
        for c in range(2):
            cur_ref[pl.ds(s * beams, beams), pl.ds(c * chunk, chunk)] = x_ref[s, c]
    for l in range(levels):
        y_ref[...] = jnp.dot(m_ref[l], cur_ref[...], preferred_element_type=jnp.float32)
        for s in range(group):
            h = (s >> l) & 1
            real = imag = 0.0
            for k in range(2):
                rows = pl.ds((k * group + s) * beams, beams)
                yr = y_ref[rows, pl.ds(0, chunk)]
                yi = y_ref[rows, pl.ds(chunk, chunk)]
                cosine, sine = cos_ref[l, k, h], sin_ref[l, k, h]
                real = real + (cosine * yr - sine * yi)
                imag = imag + (sine * yr + cosine * yi)
            cur_ref[pl.ds(s * beams, beams), pl.ds(0, chunk)] = real.astype(jnp.bfloat16)
            cur_ref[pl.ds(s * beams, beams), pl.ds(chunk, chunk)] = imag.astype(jnp.bfloat16)


def arrange(levels, beams, margin, cur_ref, l_ref, edge_ref):
    group = 2**levels
    width = group * beams
    chunk = cur_ref.shape[1] // 2
    padded = l_ref.shape[3]
    row = iota((padded, width), 0)
    lane = iota((padded, width), 1)
    beam = reverse_bits(lane // beams, levels) * beams + lane % beams
    for e in range(2):
        pick = jnp.where(row - (margin + 8 * e) == beam, 1.0, 0.0).astype(jnp.bfloat16)
        moved = jnp.dot(pick, cur_ref[...], preferred_element_type=jnp.float32)
        for m in range(l_ref.shape[1]):
            for c in range(2):
                part = moved[:, c * chunk + m * SLOT : c * chunk + (m + 1) * SLOT]
                l_ref[e, m, c] = part.astype(jnp.bfloat16)
                edge_ref[e, m, c] = jnp.broadcast_to(part[:, 0:1], (padded, LANES))


def pixels(margin, first, dest, tile_rows, range_ref, beam_ref, f0_ref, f1_ref, l_ref, edge_ref, part_ref):
    columns = range_ref.shape[2]
    slots = l_ref.shape[1]
    lanes_out = part_ref.shape[1]
    blocks = columns // lanes_out
    kappa = iota((SLOT, LANES), 0).astype(jnp.float32).astype(jnp.bfloat16)
    beta = iota((16, LANES), 0)
    for i in range(columns // LANES):
        e = i % 2
        top = 8 * i + 8 * e
        lhs = jnp.concatenate(
            [l_ref[e, m, c, top : top + 16] for m in range(slots) for c in range(2)], axis=0
        )
        edges = [
            jnp.concatenate([edge_ref[e, m, c, top : top + 16] for c in range(2)], axis=0)
            for m in range(slots)
        ]
        cols = slice(i * LANES, (i + 1) * LANES)
        ws, infos = [], []
        for row in range(tile_rows):
            y = dest * tile_rows + row
            u = range_ref[y, :, cols] - first
            f1 = f1_ref[y, :, cols]
            inside = (u >= 0) & (u < slots * SLOT)
            near = jnp.where(inside, u & (SLOT - 1), -8)
            near_b = near.astype(jnp.float32).astype(jnp.bfloat16)
            far_b = (near + 1).astype(jnp.float32).astype(jnp.bfloat16)
            w = jnp.where(
                kappa == near_b,
                (1.0 - f1).astype(jnp.bfloat16),
                jnp.where(kappa == far_b, f1.astype(jnp.bfloat16), jnp.bfloat16(0.0)),
            )
            ws.append(w)
            infos.append((u, f1, y))
        out = jnp.dot(lhs, jnp.concatenate(ws, axis=1), preferred_element_type=jnp.float32)
        for row in range(tile_rows):
            u, f1, y = infos[row]
            mine = out[:, row * LANES : (row + 1) * LANES]
            value = mine[0:32]
            for m in range(1, slots):
                value = jnp.where(u >= m * SLOT, mine[m * 32 : (m + 1) * 32], value)
            for m in range(slots):
                value = value + jnp.where(u == m * SLOT - 1, f1, 0.0) * edges[m]
            f0 = f0_ref[y, :, cols]
            low = beam_ref[y, :, cols] - (8 * i - margin)
            weight = jnp.where(beta == low, 1.0 - f0, jnp.where(beta == low + 1, f0, 0.0))
            lane0 = (i * LANES) % lanes_out
            for c in range(2):
                total = jnp.sum(value[c * 16 : c * 16 + 16] * weight, axis=0, keepdims=True)
                at = c * tile_rows * blocks + row * blocks + (i * LANES) // lanes_out
                part_ref[at : at + 1, lane0 : lane0 + LANES] = total


def compute_kernel(
    levels, margin, total, tile_rows,
    x_ref, start_ref, weight_ref, rate_ref, wave_ref, beam_ref, range_ref, frac_ref,
    out_ref,
    m_ref, cos_ref, sin_ref, cur_ref, y_ref, l_ref, edge_ref, f0_ref, f1_ref, beam3_ref, range3_ref, part_ref,
):
    group = 2**levels
    beams = x_ref.shape[2]
    chunk = x_ref.shape[-1]
    first = lax.rem(lax.axis_index("sub"), group) * chunk
    wave = wave_ref[0]
    tables(
        levels, beams, first.astype(jnp.float32), total, wave,
        start_ref, weight_ref, rate_ref, m_ref, cos_ref, sin_ref,
    )
    spread(f0_ref, frac_ref[0].astype(jnp.float32))
    spread(f1_ref, frac_ref[1].astype(jnp.float32))
    spread(beam3_ref, beam_ref[...])
    spread(range3_ref, range_ref[...])
    merge(levels, beams, x_ref, cur_ref, y_ref, m_ref, cos_ref, sin_ref)
    arrange(levels, beams, margin, cur_ref, l_ref, edge_ref)

    def one(dest, carry):
        pixels(
            margin, first, dest, tile_rows, range3_ref, beam3_ref, f0_ref, f1_ref,
            l_ref, edge_ref, part_ref,
        )
        out_ref[dest] = part_ref[...].astype(jnp.bfloat16)
        return carry

    lax.fori_loop(0, out_ref.shape[0], one, 0)


def finish_kernel(
    tile_rows,
    part_ref, wave_ref, range_ref, frac_ref,
    out_ref,
    got_ref, cart_ref, above_ref, range3_ref, f1_ref, f2_ref, send_sem, recv_sem, layer_send, layer_recv,
):
    me, layer = lax.axis_index("sub"), lax.axis_index("hgt")
    count, layers = lax.axis_size("sub"), lax.axis_size("hgt")
    lanes_out = part_ref.shape[2]
    columns = range_ref.shape[1]
    blocks = columns // lanes_out
    half = tile_rows * blocks
    has_low, has_high = layer > 0, layer < layers - 1

    barrier = pltpu.get_barrier_semaphore()
    for i in range(1, count):
        pl.semaphore_signal(
            barrier, inc=1, device_id={"sub": lax.rem(me + i, count)}, device_id_type=MESH
        )

    @pl.when(has_low)
    def _():
        pl.semaphore_signal(barrier, inc=1, device_id={"hgt": layer - 1}, device_id_type=MESH)

    @pl.when(has_high)
    def _():
        pl.semaphore_signal(barrier, inc=1, device_id={"hgt": layer + 1}, device_id_type=MESH)

    pl.semaphore_wait(barrier, count - 1 + has_low.astype(jnp.int32) + has_high.astype(jnp.int32))
    copies = []
    for i in range(1, count):
        there = lax.rem(me + i, count)
        copies.append(
            pltpu.make_async_remote_copy(
                src_ref=part_ref.at[there],
                dst_ref=got_ref.at[i],
                send_sem=send_sem.at[i],
                recv_sem=recv_sem.at[i],
                device_id={"sub": there},
                device_id_type=MESH,
            )
        )
        copies[-1].start()

    spread(range3_ref, range_ref[...])
    spread(f1_ref, frac_ref[1].astype(jnp.float32))
    spread(f2_ref, frac_ref[2].astype(jnp.float32))

    def dense(ref):
        return jnp.concatenate(
            [
                ref[me * tile_rows + row, :, b * lanes_out : (b + 1) * lanes_out]
                for row in range(tile_rows)
                for b in range(blocks)
            ],
            axis=0,
        )

    angles = wave_ref[0] * range_phase * (dense(range3_ref).astype(jnp.float32) + dense(f1_ref))
    sine, cosine = sincos(angles)
    f2 = dense(f2_ref)
    total = part_ref[me].astype(jnp.float32)
    for i in range(1, count):
        copies[i - 1].wait_recv()
        total = total + got_ref[i].astype(jnp.float32)
    real, imag = total[:half], total[half:]
    cart_ref[:half] = cosine * real - sine * imag
    cart_ref[half:] = sine * real + cosine * imag
    down = pltpu.make_async_remote_copy(
        src_ref=cart_ref,
        dst_ref=above_ref,
        send_sem=layer_send,
        recv_sem=layer_recv,
        device_id={"hgt": lax.max(layer - 1, 0)},
        device_id_type=MESH,
    )

    @pl.when(has_low)
    def _():
        down.start()

    @pl.when(has_high)
    def _():
        down.wait_recv()

    @pl.when(layer == layers - 1)
    def _():
        above_ref[...] = jnp.zeros_like(above_ref)

    for c in range(2):
        rows = slice(c * half, (c + 1) * half)
        blend = (1.0 - f2) * cart_ref[rows] + f2 * above_ref[rows]
        for row in range(tile_rows):
            for b in range(blocks):
                at = row * blocks + b
                out_ref[row, 0, c : c + 1, b * lanes_out : (b + 1) * lanes_out] = blend[at : at + 1]

    @pl.when(has_low)
    def _():
        down.wait_send()

    for copy in copies:
        copy.wait_send()


def body(
    polar_beams, band_start, band_weight, phase_rate, layer_wave, beam_map, range_map, pixel_frac
):
    count = lax.axis_size("sub")
    levels = band_start.shape[0]
    group = 2**levels
    beams, ranges = polar_beams.shape[2:]
    chunk = ranges // group
    pixel_rows, columns = beam_map.shape
    tile_rows = pixel_rows // count
    blocks = 16 // (2 * tile_rows)
    lanes_out = columns // blocks
    slots = chunk // SLOT
    width = group * beams
    margin = 2
    assert polar_beams.shape[0] == 1 and LANES * width // columns == 8
    vmem = pl.BlockSpec(memory_space=VMEM)
    smem = pl.BlockSpec(memory_space=pltpu.SMEM)

    x = pl.pallas_call(
        functools.partial(exchange_kernel, group),
        out_shape=jax.ShapeDtypeStruct((group, 2, beams, chunk), jnp.bfloat16),
        in_specs=[pl.BlockSpec(memory_space=pl.ANY)],
        out_specs=vmem,
        scratch_shapes=[
            pltpu.SemaphoreType.DMA((group,)),
            pltpu.SemaphoreType.DMA((group,)),
            pltpu.SemaphoreType.DMA,
        ],
        compiler_params=pltpu.CompilerParams(collective_id=0, has_side_effects=True),
    )(polar_beams)

    parts = pl.pallas_call(
        functools.partial(compute_kernel, levels, margin, float(ranges), tile_rows),
        out_shape=jax.ShapeDtypeStruct((count, 16, lanes_out), jnp.bfloat16),
        in_specs=[vmem, vmem, vmem, vmem, smem, vmem, vmem, vmem],
        out_specs=vmem,
        scratch_shapes=[
            VMEM((levels, 2 * width, width), jnp.bfloat16),
            VMEM((levels, 2, 2, beams, chunk), jnp.float32),
            VMEM((levels, 2, 2, beams, chunk), jnp.float32),
            VMEM((width, 2 * chunk), jnp.bfloat16),
            VMEM((2 * width, 2 * chunk), jnp.float32),
            VMEM((2, slots, 2, width + 16, SLOT), jnp.bfloat16),
            VMEM((2, slots, 2, width + 16, LANES), jnp.float32),
            VMEM((pixel_rows, 1, columns), jnp.float32),
            VMEM((pixel_rows, 1, columns), jnp.float32),
            VMEM((pixel_rows, 1, columns), jnp.int32),
            VMEM((pixel_rows, 1, columns), jnp.int32),
            VMEM((16, lanes_out), jnp.float32),
        ],
        compiler_params=pltpu.CompilerParams(vmem_limit_bytes=40 * 2**20),
    )(x, band_start, band_weight, phase_rate, layer_wave, beam_map, range_map, pixel_frac)

    return pl.pallas_call(
        functools.partial(finish_kernel, tile_rows),
        out_shape=jax.ShapeDtypeStruct((tile_rows, 1, 2, columns), jnp.float32),
        in_specs=[vmem, smem, vmem, vmem],
        out_specs=vmem,
        scratch_shapes=[
            VMEM((count, 16, lanes_out), jnp.bfloat16),
            VMEM((16, lanes_out), jnp.float32),
            VMEM((16, lanes_out), jnp.float32),
            VMEM((pixel_rows, 1, columns), jnp.int32),
            VMEM((pixel_rows, 1, columns), jnp.float32),
            VMEM((pixel_rows, 1, columns), jnp.float32),
            pltpu.SemaphoreType.DMA((count,)),
            pltpu.SemaphoreType.DMA((count,)),
            pltpu.SemaphoreType.DMA,
            pltpu.SemaphoreType.DMA,
        ],
        compiler_params=pltpu.CompilerParams(
            collective_id=1, has_side_effects=True, vmem_limit_bytes=40 * 2**20
        ),
    )(parts, layer_wave, range_map, pixel_frac)


def solution(mesh):
    in_specs = (P("hgt", None, "sub", None), P(), P(), P(), P("hgt"), P(), P(), P())
    out_specs = P("sub", "hgt", None, None)
    return jax.shard_map(body, mesh=mesh, in_specs=in_specs, out_specs=out_specs, check_vma=False)
```

time: 303 us -> 34.2 us (0.11)
  local copies, waits for them, and re-layouts: 150 us -> 2.42 us
  waiting for transfers between devices: 79.3 us -> 0 us
  other arithmetic: 47.6 us -> 0 us
  Pallas kernels: 0 us -> 30.7 us
  between operations: 15.1 us -> 0.76 us
  starting transfers between devices: 7.2 us -> 0 us
  matrix products: 3.42 us -> 0 us
    gather x8 -> x0, local copies, waits for them, and re-layouts: 111 us -> none  [body(): jnp.take(flat_polar, flat_index, axis=2)]
    unnamed x2 -> x0, waiting for transfers between devices: 58.3 us -> none
    another operation x4 -> x0, other arithmetic: 34.3 us -> none  [the longest x1 33.3 us: body(): jnp.take(flat_polar, flat_index, axis=2)]
    another operation x9 -> x0, local copies, waits for them, and re-layouts: 32.4 us -> none  [the longest x6 32.3 us: contribution(): return jnp.stack([real_part, imag_part], axis=1)]
    pallas_call x0 -> x3, Pallas kernels: none -> 30.7 us  [the longest x1 11.4 us: body(): pl.pallas_call(functools.partial(finish_kernel, tile_rows), out_shape=jax...]
    ppermute x4 -> x0, waiting for transfers between devices: 21 us -> none  [the longest x3 16.5 us: from_partner(): return lax.ppermute(value, axis, pairs)]
    ppermute x4 -> x0, starting transfers between devices: 7.19 us -> none  [the longest x3 5.91 us: from_partner(): return lax.ppermute(value, axis, pairs)]
    sub x5 -> x0, other arithmetic: 6.49 us -> none  [the longest x4 6.47 us: rotate(): cosine * real_part - sine_part * imag_part]
  transfers between devices with their start and end apart: 5 -> 0, of which waited for: 4 -> 0; matrix products, arithmetic and copies ran while one was open for 4% -> 0% of each run, Pallas kernels for 0% -> 0%
where the time goes in v1:
time: 34.2 us; the launch traced here: 33.9 us
  Pallas kernels  30.7 us (90%)
  local copies, waits for them, and re-layouts  2.42 us (7%)
  between operations  0.76 us (2%)
    pallas_call x1, Pallas kernels, body(): pl.pallas_call(functools.partial(finish_kernel, tile_rows), out_shape=jax...  11.4 us
    pallas_call x1, Pallas kernels, body(): pl.pallas_call(functools.partial(exchange_kernel, group), out_shape=jax.S...  11.2 us
    pallas_call x1, Pallas kernels, body(): pl.pallas_call(functools.partial(compute_kernel, levels, margin, float(ra...  8.17 us
    unnamed x14, local copies, waits for them, and re-layouts  2.42 us

profile of v1, /device:TPU:0, one launch (start us, length us, event | category | flops | bytes accessed | tf_op | source)
XLA Modules:
  0.0 33.9 jit_solution(2964920456671057480)
XLA Ops:
  0.7 0.8 %copy.9.weight_ref = bf16[3,2,2,16,8]{4,3,2,1,0:T(8,128)(2,1)S(1)} copy(bf16[3,2,2,16,8]{3,4,2,1,0:T(8,128)(2,1)} %param.10) | data formatting | bytes 6144 | tf_op args[2]
  1.5 0.0 copy-start.1
  1.5 0.0 copy-start.2
  1.5 0.0 copy-start.3
  1.5 0.0 copy-start.4
  1.5 0.0 copy-start.5
  1.5 11.2 %shard_map.82.x_ref = bf16[8,2,16,512]{3,2,1,0:T(8,128)(2,1)} custom-call(bf16[1,2,16,4096]{3,2,1,0:T(8,128)(2,1)} %polar_ref.1), custom_call_target="tpu_custom_call" | custom-call | tf_op jit(solution)/shard_map/pallas_call | solution.py:372
  12.7 0.0 copy-done.1
  12.7 0.0 copy-done.2
  12.7 0.0 copy-done.3
  12.7 0.0 copy-done.4
  12.8 0.0 copy-done.5
  12.8 0.0 copy-start
  12.8 0.9 %copy-done = bf16[8,2,16,512]{3,2,1,0:T(8,128)(2,1)S(1)} copy-done((bf16[8,2,16,512]{3,2,1,0:T(8,128)(2,1)S(1)}, bf16[8,2,16,512]{3,2,1,0:T(8,128)(2,1)}, u32[]{:S(2)}) %copy-start) | copy-done | bytes 262168
  13.7 8.2 %shard_map.83.part_ref = bf16[8,16,512]{2,1,0:T(8,128)(2,1)S(1)} custom-call(bf16[8,2,16,512]{3,2,1,0:T(8,128)(2,1)S(1)} %copy-done, s32[3,2,2,16]{3,2,1,0:T(2,128)S(1)} %copy-done.4, bf16[3,2,2,16,8]{4,3,2,1,0:T(8,128)(2,1)S(1)} %copy.9.weight_ref, f32[3,2,2,16]{3,2,1,0:T(2,128)S(1)} %copy-done.5, f32[1]{0:T(128)S(6)} %copy.11.wave_ref, ...), custom_call_target="tpu_custom_call" | custom-call | tf_op jit(solution)/shard_map/pallas_call | solution.py:385
  21.9 11.4 %shard_map.84 = f32[2,1,2,2048]{3,2,1,0:T(2,128)S(1)} custom-call(bf16[8,16,512]{2,1,0:T(8,128)(2,1)S(1)} %shard_map.83.part_ref, f32[1]{0:T(128)S(6)} %copy.11.wave_ref, s32[16,2048]{1,0:T(8,128)S(1)} %copy-done.2, bf16[3,16,2048]{2,1,0:T(8,128)(2,1)S(1)} %copy-done.1), custom_call_target="tpu_custom_call" | custom-call | tf_op jit(solution)/shard_map/pallas_call | solution.py:407
  33.3 0.6 %copy.12 = f32[2,1,2,2048]{3,2,1,0:T(2,128)} copy(f32[2,1,2,2048]{3,2,1,0:T(2,128)S(1)} %shard_map.84) | data formatting | bytes 65536
Async XLA Ops:
  1.5 11.2 %copy-start.1 = (bf16[3,16,2048]{2,1,0:T(8,128)(2,1)S(1)}, bf16[3,16,2048]{2,1,0:T(8,128)(2,1)}, u32[]{:S(2)}) copy-start(bf16[3,16,2048]{2,1,0:T(8,128)(2,1)} %frac_ref.3) | copy-start | bytes 589828
  1.5 11.2 %copy-start.2 = (s32[16,2048]{1,0:T(8,128)S(1)}, s32[16,2048]{1,0:T(8,128)}, u32[]{:S(2)}) copy-start(s32[16,2048]{1,0:T(8,128)} %range_ref.3) | copy-start | bytes 393220
  1.5 11.2 %copy-start.3 = (s32[16,2048]{1,0:T(8,128)S(1)}, s32[16,2048]{1,0:T(8,128)}, u32[]{:S(2)}) copy-start(s32[16,2048]{1,0:T(8,128)} %beam_ref.1) | copy-start | bytes 393220
  1.5 11.2 %copy-start.4 = (s32[3,2,2,16]{3,2,1,0:T(2,128)S(1)}, s32[3,2,2,16]{3,2,1,0:T(2,128)}, u32[]{:S(2)}) copy-start(s32[3,2,2,16]{3,2,1,0:T(2,128)} %start_ref.1) | copy-start | bytes 2308
  1.5 11.2 %copy-start.5 = (f32[3,2,2,16]{3,2,1,0:T(2,128)S(1)}, f32[3,2,2,16]{3,2,1,0:T(2,128)}, u32[]{:S(2)}) copy-start(f32[3,2,2,16]{3,2,1,0:T(2,128)} %rate_ref.1) | copy-start | bytes 2308
  12.8 1.0 %copy-start = (bf16[8,2,16,512]{3,2,1,0:T(8,128)(2,1)S(1)}, bf16[8,2,16,512]{3,2,1,0:T(8,128)(2,1)}, u32[]{:S(2)}) copy-start(bf16[8,2,16,512]{3,2,1,0:T(8,128)(2,1)} %shard_map.82.x_ref) | copy-start | bytes 786436

commit v2 on v1

--- a/solution.py
+++ b/solution.py
@@ -54,42 +54,6 @@
     return jnp.sum(jnp.where(eye, row, 0.0), axis=1, keepdims=True)
 
 
-def exchange_kernel(group, polar_ref, out_ref, send_sem, recv_sem, own_sem):
-    me = lax.axis_index("sub")
-    place = lax.rem(me, group)
-    base = me - place
-    chunk = out_ref.shape[-1]
-
-    def columns(index):
-        return pl.ds(pl.multiple_of(index * chunk, chunk), chunk)
-
-    barrier = pltpu.get_barrier_semaphore()
-    for i in range(1, group):
-        pl.semaphore_signal(
-            barrier, inc=1, device_id={"sub": base + lax.rem(place + i, group)}, device_id_type=MESH
-        )
-    pl.semaphore_wait(barrier, group - 1)
-    own = pltpu.make_async_copy(polar_ref.at[0, :, :, columns(place)], out_ref.at[place], own_sem)
-    copies = []
-    for i in range(1, group):
-        there = lax.rem(place + i, group)
-        copies.append(
-            pltpu.make_async_remote_copy(
-                src_ref=polar_ref.at[0, :, :, columns(there)],
-                dst_ref=out_ref.at[place],
-                send_sem=send_sem.at[i],
-                recv_sem=recv_sem.at[i],
-                device_id={"sub": base + there},
-                device_id_type=MESH,
-            )
-        )
-        copies[-1].start()
-    own.start()
-    own.wait()
-    for copy in copies:
-        copy.wait()
-
-
 def tables(levels, beams, first, total, wave, start_ref, weight_ref, rate_ref, m_ref, cos_ref, sin_ref):
     group = 2**levels
     width = group * beams
@@ -97,15 +61,23 @@
     lane = iota((beams, width), 1)
     lane_beam = (lane % beams).astype(jnp.float32)
     lane_sub = lane // beams
+    taps = weight_ref.shape[3]
+    eye = jnp.where(iota((beams, beams), 0) == iota((beams, beams), 1), 1.0, 0.0)
+    weights = lax.dot_general(
+        eye.astype(jnp.bfloat16),
+        weight_ref[...].reshape(levels * 4 * taps, beams),
+        (((1,), (1,)), ((), ())),
+        preferred_element_type=jnp.float32,
+    )
     pos = (iota((1, chunk), 1).astype(jnp.float32) + first + 0.5) / total
     for l in range(levels):
         for k in range(2):
             for h in range(2):
                 start = column_of(start_ref[l, k, h : h + 1].astype(jnp.float32), beams)
-                weight = weight_ref[l, k, h].astype(jnp.float32)
                 band = jnp.zeros((beams, width), jnp.float32)
-                for t in range(weight.shape[1]):
-                    band = jnp.where(lane_beam == start + t, weight[:, t : t + 1], band)
+                for t in range(taps):
+                    at = ((l * 2 + k) * 2 + h) * taps + t
+                    band = jnp.where(lane_beam == start + t, weights[:, at : at + 1], band)
                 for s in range(group):
                     if (s >> l) & 1 == h:
                         child = (s & ~(1 << l)) | (k << l)
@@ -212,86 +184,87 @@
                 part_ref[at : at + 1, lane0 : lane0 + LANES] = total
 
 
-def compute_kernel(
-    levels, margin, total, tile_rows,
+def far_first(step, count):
+    return (count // 2 + (1 - 2 * (step % 2)) * ((step + 1) // 2)) % count
+
+
+def kernel(
+    levels, margin, tile_rows,
+    polar_hbm, start_hbm, weight_hbm, rate_hbm, wave_hbm, beam_hbm, range_hbm, frac_hbm,
+    out_ref,
     x_ref, start_ref, weight_ref, rate_ref, wave_ref, beam_ref, range_ref, frac_ref,
-    out_ref,
-    m_ref, cos_ref, sin_ref, cur_ref, y_ref, l_ref, edge_ref, f0_ref, f1_ref, beam3_ref, range3_ref, part_ref,
+    m_ref, cos_ref, sin_ref, cur_ref, y_ref, l_ref, edge_ref,
+    f0_ref, f1_ref, f2_ref, beam3_ref, range3_ref, part_ref, parts_ref, got_ref, cart_ref, above_ref,
+    local_sem, x_send, x_recv, send_sem, recv_sem, layer_sem,
 ):
+    me, layer = lax.axis_index("sub"), lax.axis_index("hgt")
+    count, layers = lax.axis_size("sub"), lax.axis_size("hgt")
     group = 2**levels
-    beams = x_ref.shape[2]
-    chunk = x_ref.shape[-1]
-    first = lax.rem(lax.axis_index("sub"), group) * chunk
+    place = lax.rem(me, group)
+    base = me - place
+    beams, chunk = x_ref.shape[2:]
+    total_ranges = float(polar_hbm.shape[-1])
+    first = place * chunk
+    lanes_out = part_ref.shape[1]
+    blocks = range_ref.shape[1] // lanes_out
+    half = tile_rows * blocks
+    has_low, has_high = layer > 0, layer < layers - 1
+
+    barrier = pltpu.get_barrier_semaphore()
+    for i in range(1, count):
+        pl.semaphore_signal(
+            barrier, inc=1, device_id={"sub": lax.rem(me + i, count)}, device_id_type=MESH
+        )
+
+    @pl.when(has_low)
+    def _():
+        pl.semaphore_signal(barrier, inc=1, device_id={"hgt": layer - 1}, device_id_type=MESH)
+
+    @pl.when(has_high)
+    def _():
+        pl.semaphore_signal(barrier, inc=1, device_id={"hgt": layer + 1}, device_id_type=MESH)
+
+    def columns(index):
+        return pl.ds(pl.multiple_of(index * chunk, chunk), chunk)
+
+    pairs = [
+        (wave_hbm, wave_ref), (rate_hbm, rate_ref), (start_hbm, start_ref),
+        (weight_hbm, weight_ref), (frac_hbm, frac_ref), (beam_hbm, beam_ref),
+        (range_hbm, range_ref), (polar_hbm.at[0, :, :, columns(place)], x_ref.at[place]),
+    ]
+    locals_ = [pltpu.make_async_copy(a, b, local_sem.at[n]) for n, (a, b) in enumerate(pairs)]
+    for copy in locals_:
+        copy.start()
+    pl.semaphore_wait(barrier, count - 1 + has_low.astype(jnp.int32) + has_high.astype(jnp.int32))
+
+    exchange = []
+    for step in range(group - 1):
+        i = far_first(step, group)
+        there = lax.rem(place + i, group)
+        exchange.append(
+            pltpu.make_async_remote_copy(
+                src_ref=polar_hbm.at[0, :, :, columns(there)],
+                dst_ref=x_ref.at[place],
+                send_sem=x_send.at[i],
+                recv_sem=x_recv.at[i],
+                device_id={"sub": base + there},
+                device_id_type=MESH,
+            )
+        )
+        exchange[-1].start()
+
+    for copy in locals_:
+        copy.wait()
     wave = wave_ref[0]
     tables(
-        levels, beams, first.astype(jnp.float32), total, wave,
+        levels, beams, first.astype(jnp.float32), total_ranges, wave,
         start_ref, weight_ref, rate_ref, m_ref, cos_ref, sin_ref,
     )
     spread(f0_ref, frac_ref[0].astype(jnp.float32))
     spread(f1_ref, frac_ref[1].astype(jnp.float32))
+    spread(f2_ref, frac_ref[2].astype(jnp.float32))
     spread(beam3_ref, beam_ref[...])
     spread(range3_ref, range_ref[...])
-    merge(levels, beams, x_ref, cur_ref, y_ref, m_ref, cos_ref, sin_ref)
-    arrange(levels, beams, margin, cur_ref, l_ref, edge_ref)
-
-    def one(dest, carry):
-        pixels(
-            margin, first, dest, tile_rows, range3_ref, beam3_ref, f0_ref, f1_ref,
-            l_ref, edge_ref, part_ref,
-        )
-        out_ref[dest] = part_ref[...].astype(jnp.bfloat16)
-        return carry
-
-    lax.fori_loop(0, out_ref.shape[0], one, 0)
-
-
-def finish_kernel(
-    tile_rows,
-    part_ref, wave_ref, range_ref, frac_ref,
-    out_ref,
-    got_ref, cart_ref, above_ref, range3_ref, f1_ref, f2_ref, send_sem, recv_sem, layer_send, layer_recv,
-):
-    me, layer = lax.axis_index("sub"), lax.axis_index("hgt")
-    count, layers = lax.axis_size("sub"), lax.axis_size("hgt")
-    lanes_out = part_ref.shape[2]
-    columns = range_ref.shape[1]
-    blocks = columns // lanes_out
-    half = tile_rows * blocks
-    has_low, has_high = layer > 0, layer < layers - 1
-
-    barrier = pltpu.get_barrier_semaphore()
-    for i in range(1, count):
-        pl.semaphore_signal(
-            barrier, inc=1, device_id={"sub": lax.rem(me + i, count)}, device_id_type=MESH
-        )
-
-    @pl.when(has_low)
-    def _():
-        pl.semaphore_signal(barrier, inc=1, device_id={"hgt": layer - 1}, device_id_type=MESH)
-
-    @pl.when(has_high)
-    def _():
-        pl.semaphore_signal(barrier, inc=1, device_id={"hgt": layer + 1}, device_id_type=MESH)
-
-    pl.semaphore_wait(barrier, count - 1 + has_low.astype(jnp.int32) + has_high.astype(jnp.int32))
-    copies = []
-    for i in range(1, count):
-        there = lax.rem(me + i, count)
-        copies.append(
-            pltpu.make_async_remote_copy(
-                src_ref=part_ref.at[there],
-                dst_ref=got_ref.at[i],
-                send_sem=send_sem.at[i],
-                recv_sem=recv_sem.at[i],
-                device_id={"sub": there},
-                device_id_type=MESH,
-            )
-        )
-        copies[-1].start()
-
-    spread(range3_ref, range_ref[...])
-    spread(f1_ref, frac_ref[1].astype(jnp.float32))
-    spread(f2_ref, frac_ref[2].astype(jnp.float32))
 
     def dense(ref):
         return jnp.concatenate(
@@ -303,21 +276,52 @@
             axis=0,
         )
 
-    angles = wave_ref[0] * range_phase * (dense(range3_ref).astype(jnp.float32) + dense(f1_ref))
+    angles = wave * range_phase * (dense(range3_ref).astype(jnp.float32) + dense(f1_ref))
     sine, cosine = sincos(angles)
     f2 = dense(f2_ref)
-    total = part_ref[me].astype(jnp.float32)
-    for i in range(1, count):
-        copies[i - 1].wait_recv()
-        total = total + got_ref[i].astype(jnp.float32)
+
+    for copy in exchange:
+        copy.wait_recv()
+    merge(levels, beams, x_ref, cur_ref, y_ref, m_ref, cos_ref, sin_ref)
+    arrange(levels, beams, margin, cur_ref, l_ref, edge_ref)
+
+    def to_owner(step, i):
+        return pltpu.make_async_remote_copy(
+            src_ref=parts_ref.at[step],
+            dst_ref=got_ref.at[step],
+            send_sem=send_sem.at[step],
+            recv_sem=recv_sem.at[step],
+            device_id={"sub": lax.rem(me + i, count)},
+            device_id_type=MESH,
+        )
+
+    def one(step, carry):
+        i = far_first(step, count)
+        pixels(
+            margin, first, lax.rem(me + i, count), tile_rows, range3_ref, beam3_ref, f0_ref, f1_ref,
+            l_ref, edge_ref, part_ref,
+        )
+        parts_ref[step] = part_ref[...].astype(jnp.bfloat16)
+
+        @pl.when(step < count - 1)
+        def _():
+            to_owner(step, i).start()
+
+        return carry
+
+    lax.fori_loop(0, count, one, 0)
+    total = part_ref[...]
+    for step in range(count - 1):
+        to_owner(step, far_first(step, count)).wait_recv()
+        total = total + got_ref[step].astype(jnp.float32)
     real, imag = total[:half], total[half:]
     cart_ref[:half] = cosine * real - sine * imag
     cart_ref[half:] = sine * real + cosine * imag
     down = pltpu.make_async_remote_copy(
         src_ref=cart_ref,
         dst_ref=above_ref,
-        send_sem=layer_send,
-        recv_sem=layer_recv,
+        send_sem=layer_sem.at[0],
+        recv_sem=layer_sem.at[1],
         device_id={"hgt": lax.max(layer - 1, 0)},
         device_id_type=MESH,
     )
@@ -346,8 +350,10 @@
     def _():
         down.wait_send()
 
-    for copy in copies:
+    for copy in exchange:
         copy.wait_send()
+    for step in range(count - 1):
+        to_owner(step, far_first(step, count)).wait_send()
 
 
 def body(
@@ -364,30 +370,22 @@
     lanes_out = columns // blocks
     slots = chunk // SLOT
     width = group * beams
-    margin = 2
     assert polar_beams.shape[0] == 1 and LANES * width // columns == 8
-    vmem = pl.BlockSpec(memory_space=VMEM)
-    smem = pl.BlockSpec(memory_space=pltpu.SMEM)
-
-    x = pl.pallas_call(
-        functools.partial(exchange_kernel, group),
-        out_shape=jax.ShapeDtypeStruct((group, 2, beams, chunk), jnp.bfloat16),
-        in_specs=[pl.BlockSpec(memory_space=pl.ANY)],
-        out_specs=vmem,
+    tap_rows = jnp.swapaxes(band_weight, 3, 4)
+    small = [band_start, tap_rows, phase_rate]
+    maps = [beam_map, range_map, pixel_frac]
+    rows3 = (pixel_rows, 1, columns)
+    dma = pltpu.SemaphoreType.DMA
+    return pl.pallas_call(
+        functools.partial(kernel, levels, 2, tile_rows),
+        out_shape=jax.ShapeDtypeStruct((tile_rows, 1, 2, columns), jnp.float32),
+        in_specs=[pl.BlockSpec(memory_space=pl.ANY)] * 8,
+        out_specs=pl.BlockSpec(memory_space=VMEM),
         scratch_shapes=[
-            pltpu.SemaphoreType.DMA((group,)),
-            pltpu.SemaphoreType.DMA((group,)),
-            pltpu.SemaphoreType.DMA,
-        ],
-        compiler_params=pltpu.CompilerParams(collective_id=0, has_side_effects=True),
-    )(polar_beams)
-
-    parts = pl.pallas_call(
-        functools.partial(compute_kernel, levels, margin, float(ranges), tile_rows),
-        out_shape=jax.ShapeDtypeStruct((count, 16, lanes_out), jnp.bfloat16),
-        in_specs=[vmem, vmem, vmem, vmem, smem, vmem, vmem, vmem],
-        out_specs=vmem,
-        scratch_shapes=[
+            VMEM((group, 2, beams, chunk), jnp.bfloat16),
+            *[VMEM(a.shape, a.dtype) for a in small],
+            pltpu.SMEM((1,), jnp.float32),
+            *[VMEM(a.shape, a.dtype) for a in maps],
             VMEM((levels, 2 * width, width), jnp.bfloat16),
             VMEM((levels, 2, 2, beams, chunk), jnp.float32),
             VMEM((levels, 2, 2, beams, chunk), jnp.float32),
@@ -395,36 +393,29 @@
             VMEM((2 * width, 2 * chunk), jnp.float32),
             VMEM((2, slots, 2, width + 16, SLOT), jnp.bfloat16),
             VMEM((2, slots, 2, width + 16, LANES), jnp.float32),
-            VMEM((pixel_rows, 1, columns), jnp.float32),
-            VMEM((pixel_rows, 1, columns), jnp.float32),
-            VMEM((pixel_rows, 1, columns), jnp.int32),
-            VMEM((pixel_rows, 1, columns), jnp.int32),
+            VMEM(rows3, jnp.float32),
+            VMEM(rows3, jnp.float32),
+            VMEM(rows3, jnp.float32),
+            VMEM(rows3, jnp.int32),
+            VMEM(rows3, jnp.int32),
             VMEM((16, lanes_out), jnp.float32),
-        ],
-        compiler_params=pltpu.CompilerParams(vmem_limit_bytes=40 * 2**20),
-    )(x, band_start, band_weight, phase_rate, layer_wave, beam_map, range_map, pixel_frac)
-
-    return pl.pallas_call(
-        functools.partial(finish_kernel, tile_rows),
-        out_shape=jax.ShapeDtypeStruct((tile_rows, 1, 2, columns), jnp.float32),
-        in_specs=[vmem, smem, vmem, vmem],
-        out_specs=vmem,
-        scratch_shapes=[
+            VMEM((count, 16, lanes_out), jnp.bfloat16),
             VMEM((count, 16, lanes_out), jnp.bfloat16),
             VMEM((16, lanes_out), jnp.float32),
             VMEM((16, lanes_out), jnp.float32),
-            VMEM((pixel_rows, 1, columns), jnp.int32),
-            VMEM((pixel_rows, 1, columns), jnp.float32),
-            VMEM((pixel_rows, 1, columns), jnp.float32),
-            pltpu.SemaphoreType.DMA((count,)),
-            pltpu.SemaphoreType.DMA((count,)),
-            pltpu.SemaphoreType.DMA,
-            pltpu.SemaphoreType.DMA,
+            dma((8,)),
+            dma((group,)),
+            dma((group,)),
+            dma((count,)),
+            dma((count,)),
+            dma((2,)),
         ],
         compiler_params=pltpu.CompilerParams(
-            collective_id=1, has_side_effects=True, vmem_limit_bytes=40 * 2**20
+            collective_id=0, has_side_effects=True, vmem_limit_bytes=63 * 2**20 + 2**19
         ),
-    )(parts, layer_wave, range_map, pixel_frac)
+    )(
+        polar_beams, band_start, tap_rows, phase_rate, layer_wave, beam_map, range_map, pixel_frac
+    )
 
 
 def solution(mesh):

time: 34.2 us -> 28.1 us (0.82)
  Pallas kernels: 30.7 us -> 25.9 us
  local copies, waits for them, and re-layouts: 2.42 us -> 1.38 us
    pallas_call x3 -> x1, Pallas kernels: 30.7 us -> 25.9 us  [body(): pl.pallas_call(functools.partial(kernel, levels, 2, tile_rows), out_shape...]
    unnamed x14 -> x1, local copies, waits for them, and re-layouts: 2.42 us -> 1.38 us
where the time goes in v2:
time: 28.1 us; the launch traced here: 27.9 us
  Pallas kernels  25.9 us (92%)
  local copies, waits for them, and re-layouts  1.38 us (5%)
  between operations  0.66 us (2%)
    pallas_call x1, Pallas kernels, body(): pl.pallas_call(functools.partial(kernel, levels, 2, tile_rows), out_shape...  25.9 us
    unnamed x1, local copies, waits for them, and re-layouts  1.38 us

profile of v2, /device:TPU:0, one launch (start us, length us, event | category | flops | bytes accessed | tf_op | source)
XLA Modules:
  0.0 27.9 jit_solution(12551012877614709389)
XLA Ops:
  0.7 25.9 %shard_map.82 = f32[2,1,2,2048]{3,2,1,0:T(2,128)} custom-call(bf16[1,2,16,4096]{3,2,1,0:T(8,128)(2,1)} %polar_hbm.1, s32[3,2,2,16]{3,2,1,0:T(2,128)} %start_hbm.1, bf16[3,2,2,8,16]{4,3,2,1,0:T(8,128)(2,1)} %bitcast.1, f32[3,2,2,16]{3,2,1,0:T(2,128)} %rate_hbm.1, f32[1]{0:T(128)S(6)} %copy.10.wave_hbm, s32[16,2048]{1,0:T(8,128)} %beam_hbm.1, ...), custom_call_target="tpu_custom_call" | custom-call | tf_op jit(solution)/shard_map/pallas_call | solution.py:379
  26.5 1.4 %copy.11 = f32[2,1,2,2048]{3,2,1,0:T(2,128)} copy(f32[2,1,2,2048]{3,2,1,0:T(2,128)} %shard_map.82) | data formatting | bytes 65536

commit v3 on v2

--- a/solution.py
+++ b/solution.py
@@ -1,4 +1,5 @@
 import functools
+import math
 
 import jax
 import jax.numpy as jnp
@@ -128,15 +129,36 @@
             for c in range(2):
                 part = moved[:, c * chunk + m * SLOT : c * chunk + (m + 1) * SLOT]
                 l_ref[e, m, c] = part.astype(jnp.bfloat16)
-                edge_ref[e, m, c] = jnp.broadcast_to(part[:, 0:1], (padded, LANES))
-
-
-def pixels(margin, first, dest, tile_rows, range_ref, beam_ref, f0_ref, f1_ref, l_ref, edge_ref, part_ref):
+                if m + 1 < l_ref.shape[1]:
+                    edge_ref[e, m, c] = jnp.broadcast_to(part[:, SLOT - 1 :], (padded, LANES))
+
+
+def near_sample(u, slots):
+    near = u
+    for m in range(1, slots):
+        near = near - jnp.where(u >= m * SLOT - 1, SLOT, 0)
+    return near
+
+
+def interpolation(first, slots, i, y, range_ref, f1_ref):
+    cols = slice(i * LANES, (i + 1) * LANES)
+    kappa = iota((SLOT, LANES), 0).astype(jnp.float32).astype(jnp.bfloat16)
+    near = near_sample(range_ref[y, :, cols] - first, slots)
+    f1 = f1_ref[y, :, cols]
+    near_b = near.astype(jnp.float32).astype(jnp.bfloat16)
+    far_b = (near + 1).astype(jnp.float32).astype(jnp.bfloat16)
+    return jnp.where(
+        kappa == near_b,
+        (1.0 - f1).astype(jnp.bfloat16),
+        jnp.where(kappa == far_b, f1.astype(jnp.bfloat16), jnp.bfloat16(0.0)),
+    )
+
+
+def pixels(margin, first, dest, step, tile_rows, range_ref, beam_ref, f0_ref, f1_ref, l_ref, edge_ref, w_ref, part_ref):
     columns = range_ref.shape[2]
     slots = l_ref.shape[1]
     lanes_out = part_ref.shape[1]
     blocks = columns // lanes_out
-    kappa = iota((SLOT, LANES), 0).astype(jnp.float32).astype(jnp.bfloat16)
     beta = iota((16, LANES), 0)
     for i in range(columns // LANES):
         e = i % 2
@@ -146,34 +168,30 @@
         )
         edges = [
             jnp.concatenate([edge_ref[e, m, c, top : top + 16] for c in range(2)], axis=0)
-            for m in range(slots)
+            for m in range(slots - 1)
         ]
         cols = slice(i * LANES, (i + 1) * LANES)
-        ws, infos = [], []
+        if w_ref is None:
+            weights = jnp.concatenate(
+                [
+                    interpolation(first, slots, i, dest * tile_rows + row, range_ref, f1_ref)
+                    for row in range(tile_rows)
+                ],
+                axis=1,
+            )
+        else:
+            weights = w_ref[step, i]
+        out = jnp.dot(lhs, weights, preferred_element_type=jnp.float32)
         for row in range(tile_rows):
             y = dest * tile_rows + row
             u = range_ref[y, :, cols] - first
             f1 = f1_ref[y, :, cols]
-            inside = (u >= 0) & (u < slots * SLOT)
-            near = jnp.where(inside, u & (SLOT - 1), -8)
-            near_b = near.astype(jnp.float32).astype(jnp.bfloat16)
-            far_b = (near + 1).astype(jnp.float32).astype(jnp.bfloat16)
-            w = jnp.where(
-                kappa == near_b,
-                (1.0 - f1).astype(jnp.bfloat16),
-                jnp.where(kappa == far_b, f1.astype(jnp.bfloat16), jnp.bfloat16(0.0)),
-            )
-            ws.append(w)
-            infos.append((u, f1, y))
-        out = jnp.dot(lhs, jnp.concatenate(ws, axis=1), preferred_element_type=jnp.float32)
-        for row in range(tile_rows):
-            u, f1, y = infos[row]
             mine = out[:, row * LANES : (row + 1) * LANES]
             value = mine[0:32]
             for m in range(1, slots):
-                value = jnp.where(u >= m * SLOT, mine[m * 32 : (m + 1) * 32], value)
-            for m in range(slots):
-                value = value + jnp.where(u == m * SLOT - 1, f1, 0.0) * edges[m]
+                value = jnp.where(u >= m * SLOT - 1, mine[m * 32 : (m + 1) * 32], value)
+            for m in range(1, slots):
+                value = value + jnp.where(u == m * SLOT - 1, 1.0 - f1, 0.0) * edges[m - 1]
             f0 = f0_ref[y, :, cols]
             low = beam_ref[y, :, cols] - (8 * i - margin)
             weight = jnp.where(beta == low, 1.0 - f0, jnp.where(beta == low + 1, f0, 0.0))
@@ -189,12 +207,12 @@
 
 
 def kernel(
-    levels, margin, tile_rows,
+    levels, margin, tile_rows, ahead,
     polar_hbm, start_hbm, weight_hbm, rate_hbm, wave_hbm, beam_hbm, range_hbm, frac_hbm,
     out_ref,
     x_ref, start_ref, weight_ref, rate_ref, wave_ref, beam_ref, range_ref, frac_ref,
     m_ref, cos_ref, sin_ref, cur_ref, y_ref, l_ref, edge_ref,
-    f0_ref, f1_ref, f2_ref, beam3_ref, range3_ref, part_ref, parts_ref, got_ref, cart_ref, above_ref,
+    f0_ref, f1_ref, f2_ref, beam3_ref, range3_ref, part_ref, parts_ref, got_ref, cart_ref, above_ref, w_ref,
     local_sem, x_send, x_recv, send_sem, recv_sem, layer_sem,
 ):
     me, layer = lax.axis_index("sub"), lax.axis_index("hgt")
@@ -280,6 +298,17 @@
     sine, cosine = sincos(angles)
     f2 = dense(f2_ref)
 
+    def weights_of(step, carry):
+        dest = lax.rem(me + far_first(step, count), count)
+        for i in range(w_ref.shape[1]):
+            for row in range(tile_rows):
+                w_ref[step, i, :, row * LANES : (row + 1) * LANES] = interpolation(
+                    first, l_ref.shape[1], i, dest * tile_rows + row, range3_ref, f1_ref
+                )
+        return carry
+
+    if ahead:
+        lax.fori_loop(0, count, weights_of, 0)
     for copy in exchange:
         copy.wait_recv()
     merge(levels, beams, x_ref, cur_ref, y_ref, m_ref, cos_ref, sin_ref)
@@ -298,8 +327,8 @@
     def one(step, carry):
         i = far_first(step, count)
         pixels(
-            margin, first, lax.rem(me + i, count), tile_rows, range3_ref, beam3_ref, f0_ref, f1_ref,
-            l_ref, edge_ref, part_ref,
+            margin, first, lax.rem(me + i, count), step, tile_rows, range3_ref, beam3_ref, f0_ref,
+            f1_ref, l_ref, edge_ref, w_ref if ahead else None, part_ref,
         )
         parts_ref[step] = part_ref[...].astype(jnp.bfloat16)
 
@@ -376,8 +405,12 @@
     maps = [beam_map, range_map, pixel_frac]
     rows3 = (pixel_rows, 1, columns)
     dma = pltpu.SemaphoreType.DMA
+    w_shape = (count, columns // LANES, SLOT, tile_rows * LANES)
+    ahead = 2 * math.prod(w_shape) <= 24 * 2**20
+    if not ahead:
+        w_shape = (1, 1, 16, LANES)
     return pl.pallas_call(
-        functools.partial(kernel, levels, 2, tile_rows),
+        functools.partial(kernel, levels, 2, tile_rows, ahead),
         out_shape=jax.ShapeDtypeStruct((tile_rows, 1, 2, columns), jnp.float32),
         in_specs=[pl.BlockSpec(memory_space=pl.ANY)] * 8,
         out_specs=pl.BlockSpec(memory_space=VMEM),
@@ -392,7 +425,7 @@
             VMEM((width, 2 * chunk), jnp.bfloat16),
             VMEM((2 * width, 2 * chunk), jnp.float32),
             VMEM((2, slots, 2, width + 16, SLOT), jnp.bfloat16),
-            VMEM((2, slots, 2, width + 16, LANES), jnp.float32),
+            VMEM((2, max(slots - 1, 1), 2, width + 16, LANES), jnp.float32),
             VMEM(rows3, jnp.float32),
             VMEM(rows3, jnp.float32),
             VMEM(rows3, jnp.float32),
@@ -403,6 +436,7 @@
             VMEM((count, 16, lanes_out), jnp.bfloat16),
             VMEM((16, lanes_out), jnp.float32),
             VMEM((16, lanes_out), jnp.float32),
+            VMEM(w_shape, jnp.bfloat16),
             dma((8,)),
             dma((group,)),
             dma((group,)),
@@ -411,7 +445,7 @@
             dma((2,)),
         ],
         compiler_params=pltpu.CompilerParams(
-            collective_id=0, has_side_effects=True, vmem_limit_bytes=63 * 2**20 + 2**19
+            collective_id=0, has_side_effects=True, vmem_limit_bytes=254 * 2**18
         ),
     )(
         polar_beams, band_start, tap_rows, phase_rate, layer_wave, beam_map, range_map, pixel_frac

time: 28.1 us -> 26.6 us (0.947)
  Pallas kernels: 25.9 us -> 24.4 us
    pallas_call x1, Pallas kernels: 25.9 us -> 24.4 us  [body(): pl.pallas_call(functools.partial(kernel, levels, 2, tile_rows, ahead), ou...]
where the time goes in v3:
time: 26.6 us; the launch traced here: 26.4 us
  Pallas kernels  24.4 us (92%)
  local copies, waits for them, and re-layouts  1.38 us (5%)
  between operations  0.66 us (2%)
    pallas_call x1, Pallas kernels, body(): pl.pallas_call(functools.partial(kernel, levels, 2, tile_rows, ahead), ou...  24.4 us
    unnamed x1, local copies, waits for them, and re-layouts  1.38 us

profile of v3, /device:TPU:0, one launch (start us, length us, event | category | flops | bytes accessed | tf_op | source)
XLA Modules:
  0.0 26.4 jit_solution(4787321309970414663)
XLA Ops:
  0.7 24.4 %shard_map.82 = f32[2,1,2,2048]{3,2,1,0:T(2,128)} custom-call(bf16[1,2,16,4096]{3,2,1,0:T(8,128)(2,1)} %polar_hbm.1, s32[3,2,2,16]{3,2,1,0:T(2,128)} %start_hbm.1, bf16[3,2,2,8,16]{4,3,2,1,0:T(8,128)(2,1)} %bitcast.1, f32[3,2,2,16]{3,2,1,0:T(2,128)} %rate_hbm.1, f32[1]{0:T(128)S(6)} %copy.10.wave_hbm, s32[16,2048]{1,0:T(8,128)} %beam_hbm.1, ...), custom_call_target="tpu_custom_call" | custom-call | tf_op jit(solution)/shard_map/pallas_call | solution.py:412
  25.0 1.4 %copy.11 = f32[2,1,2,2048]{3,2,1,0:T(2,128)} copy(f32[2,1,2,2048]{3,2,1,0:T(2,128)} %shard_map.82) | data formatting | bytes 65536

commit v4 on v3

--- a/solution.py
+++ b/solution.py
@@ -91,13 +91,12 @@
                 sin_ref[l, k, h] = sine
 
 
-def merge(levels, beams, x_ref, cur_ref, y_ref, m_ref, cos_ref, sin_ref):
+def merge(levels, beams, m, x_ref, cur_ref, y_ref, m_ref, cos_ref, sin_ref):
     group = 2**levels
-    width = group * beams
-    chunk = x_ref.shape[-1]
+    part = pl.ds(m * SLOT, SLOT)
     for s in range(group):
         for c in range(2):
-            cur_ref[pl.ds(s * beams, beams), pl.ds(c * chunk, chunk)] = x_ref[s, c]
+            cur_ref[pl.ds(s * beams, beams), pl.ds(c * SLOT, SLOT)] = x_ref[s, c, :, part]
     for l in range(levels):
         y_ref[...] = jnp.dot(m_ref[l], cur_ref[...], preferred_element_type=jnp.float32)
         for s in range(group):
@@ -105,19 +104,18 @@
             real = imag = 0.0
             for k in range(2):
                 rows = pl.ds((k * group + s) * beams, beams)
-                yr = y_ref[rows, pl.ds(0, chunk)]
-                yi = y_ref[rows, pl.ds(chunk, chunk)]
-                cosine, sine = cos_ref[l, k, h], sin_ref[l, k, h]
+                yr = y_ref[rows, pl.ds(0, SLOT)]
+                yi = y_ref[rows, pl.ds(SLOT, SLOT)]
+                cosine, sine = cos_ref[l, k, h, :, part], sin_ref[l, k, h, :, part]
                 real = real + (cosine * yr - sine * yi)
                 imag = imag + (sine * yr + cosine * yi)
-            cur_ref[pl.ds(s * beams, beams), pl.ds(0, chunk)] = real.astype(jnp.bfloat16)
-            cur_ref[pl.ds(s * beams, beams), pl.ds(chunk, chunk)] = imag.astype(jnp.bfloat16)
-
-
-def arrange(levels, beams, margin, cur_ref, l_ref, edge_ref):
+            cur_ref[pl.ds(s * beams, beams), pl.ds(0, SLOT)] = real.astype(jnp.bfloat16)
+            cur_ref[pl.ds(s * beams, beams), pl.ds(SLOT, SLOT)] = imag.astype(jnp.bfloat16)
+
+
+def arrange(levels, beams, margin, m, cur_ref, l_ref, edge_ref):
     group = 2**levels
     width = group * beams
-    chunk = cur_ref.shape[1] // 2
     padded = l_ref.shape[3]
     row = iota((padded, width), 0)
     lane = iota((padded, width), 1)
@@ -125,12 +123,11 @@
     for e in range(2):
         pick = jnp.where(row - (margin + 8 * e) == beam, 1.0, 0.0).astype(jnp.bfloat16)
         moved = jnp.dot(pick, cur_ref[...], preferred_element_type=jnp.float32)
-        for m in range(l_ref.shape[1]):
-            for c in range(2):
-                part = moved[:, c * chunk + m * SLOT : c * chunk + (m + 1) * SLOT]
-                l_ref[e, m, c] = part.astype(jnp.bfloat16)
-                if m + 1 < l_ref.shape[1]:
-                    edge_ref[e, m, c] = jnp.broadcast_to(part[:, SLOT - 1 :], (padded, LANES))
+        for c in range(2):
+            part = moved[:, c * SLOT : (c + 1) * SLOT]
+            l_ref[e, m, c] = part.astype(jnp.bfloat16)
+            if m + 1 < l_ref.shape[1]:
+                edge_ref[e, m, c] = jnp.broadcast_to(part[:, SLOT - 1 :], (padded, LANES))
 
 
 def near_sample(u, slots):
@@ -154,12 +151,22 @@
     )
 
 
-def pixels(margin, first, dest, step, tile_rows, range_ref, beam_ref, f0_ref, f1_ref, l_ref, edge_ref, w_ref, part_ref):
+def beam_weights(margin, i, y, beam_ref, f0_ref):
+    cols = slice(i * LANES, (i + 1) * LANES)
+    beta = iota((16, LANES), 0)
+    f0 = f0_ref[y, :, cols]
+    low = beam_ref[y, :, cols] - (8 * i - margin)
+    return jnp.where(beta == low, 1.0 - f0, jnp.where(beta == low + 1, f0, 0.0))
+
+
+def pixels(
+    margin, first, dest, step, tile_rows,
+    range_ref, beam_ref, f0_ref, f1_ref, l_ref, edge_ref, w_ref, b_ref, part_ref,
+):
     columns = range_ref.shape[2]
     slots = l_ref.shape[1]
     lanes_out = part_ref.shape[1]
     blocks = columns // lanes_out
-    beta = iota((16, LANES), 0)
     for i in range(columns // LANES):
         e = i % 2
         top = 8 * i + 8 * e
@@ -192,9 +199,10 @@
                 value = jnp.where(u >= m * SLOT - 1, mine[m * 32 : (m + 1) * 32], value)
             for m in range(1, slots):
                 value = value + jnp.where(u == m * SLOT - 1, 1.0 - f1, 0.0) * edges[m - 1]
-            f0 = f0_ref[y, :, cols]
-            low = beam_ref[y, :, cols] - (8 * i - margin)
-            weight = jnp.where(beta == low, 1.0 - f0, jnp.where(beta == low + 1, f0, 0.0))
+            if w_ref is None:
+                weight = beam_weights(margin, i, y, beam_ref, f0_ref)
+            else:
+                weight = b_ref[step, i, row]
             lane0 = (i * LANES) % lanes_out
             for c in range(2):
                 total = jnp.sum(value[c * 16 : c * 16 + 16] * weight, axis=0, keepdims=True)
@@ -212,7 +220,7 @@
     out_ref,
     x_ref, start_ref, weight_ref, rate_ref, wave_ref, beam_ref, range_ref, frac_ref,
     m_ref, cos_ref, sin_ref, cur_ref, y_ref, l_ref, edge_ref,
-    f0_ref, f1_ref, f2_ref, beam3_ref, range3_ref, part_ref, parts_ref, got_ref, cart_ref, above_ref, w_ref,
+    f0_ref, f1_ref, f2_ref, beam3_ref, range3_ref, part_ref, parts_ref, got_ref, cart_ref, above_ref, w_ref, b_ref,
     local_sem, x_send, x_recv, send_sem, recv_sem, layer_sem,
 ):
     me, layer = lax.axis_index("sub"), lax.axis_index("hgt")
@@ -255,21 +263,24 @@
         copy.start()
     pl.semaphore_wait(barrier, count - 1 + has_low.astype(jnp.int32) + has_high.astype(jnp.int32))
 
+    slots = l_ref.shape[1]
     exchange = []
-    for step in range(group - 1):
-        i = far_first(step, group)
-        there = lax.rem(place + i, group)
-        exchange.append(
-            pltpu.make_async_remote_copy(
-                src_ref=polar_hbm.at[0, :, :, columns(there)],
-                dst_ref=x_ref.at[place],
-                send_sem=x_send.at[i],
-                recv_sem=x_recv.at[i],
+    for m in range(slots):
+        exchange.append([])
+        for step in range(group - 1):
+            i = far_first(step, group)
+            there = lax.rem(place + i, group)
+            source = pl.ds(pl.multiple_of(there * chunk + m * SLOT, SLOT), SLOT)
+            copy = pltpu.make_async_remote_copy(
+                src_ref=polar_hbm.at[0, :, :, source],
+                dst_ref=x_ref.at[place, :, :, pl.ds(m * SLOT, SLOT)],
+                send_sem=x_send.at[m, i],
+                recv_sem=x_recv.at[m, i],
                 device_id={"sub": base + there},
                 device_id_type=MESH,
             )
-        )
-        exchange[-1].start()
+            exchange[m].append(copy)
+            copy.start()
 
     for copy in locals_:
         copy.wait()
@@ -303,16 +314,20 @@
         for i in range(w_ref.shape[1]):
             for row in range(tile_rows):
                 w_ref[step, i, :, row * LANES : (row + 1) * LANES] = interpolation(
-                    first, l_ref.shape[1], i, dest * tile_rows + row, range3_ref, f1_ref
+                    first, slots, i, dest * tile_rows + row, range3_ref, f1_ref
+                )
+                b_ref[step, i, row] = beam_weights(
+                    margin, i, dest * tile_rows + row, beam3_ref, f0_ref
                 )
         return carry
 
     if ahead:
         lax.fori_loop(0, count, weights_of, 0)
-    for copy in exchange:
-        copy.wait_recv()
-    merge(levels, beams, x_ref, cur_ref, y_ref, m_ref, cos_ref, sin_ref)
-    arrange(levels, beams, margin, cur_ref, l_ref, edge_ref)
+    for m in range(slots):
+        for copy in exchange[m]:
+            copy.wait_recv()
+        merge(levels, beams, m, x_ref, cur_ref, y_ref, m_ref, cos_ref, sin_ref)
+        arrange(levels, beams, margin, m, cur_ref, l_ref, edge_ref)
 
     def to_owner(step, i):
         return pltpu.make_async_remote_copy(
@@ -328,7 +343,7 @@
         i = far_first(step, count)
         pixels(
             margin, first, lax.rem(me + i, count), step, tile_rows, range3_ref, beam3_ref, f0_ref,
-            f1_ref, l_ref, edge_ref, w_ref if ahead else None, part_ref,
+            f1_ref, l_ref, edge_ref, w_ref if ahead else None, b_ref, part_ref,
         )
         parts_ref[step] = part_ref[...].astype(jnp.bfloat16)
 
@@ -379,8 +394,9 @@
     def _():
         down.wait_send()
 
-    for copy in exchange:
-        copy.wait_send()
+    for copies in exchange:
+        for copy in copies:
+            copy.wait_send()
     for step in range(count - 1):
         to_owner(step, far_first(step, count)).wait_send()
 
@@ -407,8 +423,9 @@
     dma = pltpu.SemaphoreType.DMA
     w_shape = (count, columns // LANES, SLOT, tile_rows * LANES)
     ahead = 2 * math.prod(w_shape) <= 24 * 2**20
+    b_shape = (*w_shape[:2], tile_rows, 16, LANES)
     if not ahead:
-        w_shape = (1, 1, 16, LANES)
+        w_shape, b_shape = (1, 1, 16, LANES), (1, 1, 1, 16, LANES)
     return pl.pallas_call(
         functools.partial(kernel, levels, 2, tile_rows, ahead),
         out_shape=jax.ShapeDtypeStruct((tile_rows, 1, 2, columns), jnp.float32),
@@ -422,8 +439,8 @@
             VMEM((levels, 2 * width, width), jnp.bfloat16),
             VMEM((levels, 2, 2, beams, chunk), jnp.float32),
             VMEM((levels, 2, 2, beams, chunk), jnp.float32),
-            VMEM((width, 2 * chunk), jnp.bfloat16),
-            VMEM((2 * width, 2 * chunk), jnp.float32),
+            VMEM((width, 2 * SLOT), jnp.bfloat16),
+            VMEM((2 * width, 2 * SLOT), jnp.float32),
             VMEM((2, slots, 2, width + 16, SLOT), jnp.bfloat16),
             VMEM((2, max(slots - 1, 1), 2, width + 16, LANES), jnp.float32),
             VMEM(rows3, jnp.float32),
@@ -437,15 +454,16 @@
             VMEM((16, lanes_out), jnp.float32),
             VMEM((16, lanes_out), jnp.float32),
             VMEM(w_shape, jnp.bfloat16),
+            VMEM(b_shape, jnp.float32),
             dma((8,)),
-            dma((group,)),
-            dma((group,)),
+            dma((slots, group)),
+            dma((slots, group)),
             dma((count,)),
             dma((count,)),
             dma((2,)),
         ],
         compiler_params=pltpu.CompilerParams(
-            collective_id=0, has_side_effects=True, vmem_limit_bytes=254 * 2**18
+            collective_id=0, has_side_effects=True, vmem_limit_bytes=63 * 2**20 + 2**19
         ),
     )(
         polar_beams, band_start, tap_rows, phase_rate, layer_wave, beam_map, range_map, pixel_frac

time: 26.6 us -> 26.3 us (0.989)
  Pallas kernels: 24.4 us -> 24 us
    pallas_call x1, Pallas kernels: 24.4 us -> 24 us  [body(): pl.pallas_call(functools.partial(kernel, levels, 2, tile_rows, ahead), ou...]
where the time goes in v4:
time: 26.3 us; the launch traced here: 26.1 us
  Pallas kernels  24 us (91%)
  local copies, waits for them, and re-layouts  1.38 us (5%)
  between operations  0.66 us (3%)
    pallas_call x1, Pallas kernels, body(): pl.pallas_call(functools.partial(kernel, levels, 2, tile_rows, ahead), ou...  24 us
    unnamed x1, local copies, waits for them, and re-layouts  1.38 us

profile of v4, /device:TPU:0, one launch (start us, length us, event | category | flops | bytes accessed | tf_op | source)
XLA Modules:
  0.0 26.1 jit_solution(6867518139756458303)
XLA Ops:
  0.7 24.0 %shard_map.82 = f32[2,1,2,2048]{3,2,1,0:T(2,128)} custom-call(bf16[1,2,16,4096]{3,2,1,0:T(8,128)(2,1)} %polar_hbm.1, s32[3,2,2,16]{3,2,1,0:T(2,128)} %start_hbm.1, bf16[3,2,2,8,16]{4,3,2,1,0:T(8,128)(2,1)} %bitcast.1, f32[3,2,2,16]{3,2,1,0:T(2,128)} %rate_hbm.1, f32[1]{0:T(128)S(6)} %copy.10.wave_hbm, s32[16,2048]{1,0:T(8,128)} %beam_hbm.1, ...), custom_call_target="tpu_custom_call" | custom-call | tf_op jit(solution)/shard_map/pallas_call | solution.py:429
  24.7 1.4 %copy.11 = f32[2,1,2,2048]{3,2,1,0:T(2,128)} copy(f32[2,1,2,2048]{3,2,1,0:T(2,128)} %shard_map.82) | data formatting | bytes 65536
